TPU v7x, 32 devices: a whole 2x2x4 slice. The times are simulated.
32 devices in a mesh: seq: 8 (over z, x), rep: 4 (over y, core).
Axes of the slice: x: 2, y: 2, z: 4, core: 2. Of those that a mesh axis runs over, the one named last changes fastest.
Arguments:
- hidden: bfloat16 [2, 512, 1024], P(None, 'seq'), may hold values from -6 to 6
- w_query: bfloat16 [1024, 1024], P(None, 'rep'), may hold values from -0.1875 to 0.1875
- w_key: bfloat16 [1024, 1024], P(None, 'rep'), may hold values from -0.4375 to 0.4375
- w_value: bfloat16 [1024, 1024], P(None, 'rep'), may hold values from -0.1875 to 0.1875
- w_out: bfloat16 [1024, 1024], P('rep'), may hold values from -0.1875 to 0.1875
- norm_gain: float32 [1024], P('rep'), may hold values from 0.1 to 1.9
- norm_bias: float32 [1024], P('rep'), may hold values from -3 to 3
- kv_cache: bfloat16 [8, 8704, 512], P('seq', None, 'rep'), may hold values from -300 to 300
- cache_lengths: int32 [2], replicated, may hold values from 1 to 8192, as said below
- append_counts: int32 [2], replicated, may hold values from 128 to 512, as said below
Outputs:
- out_hidden: bfloat16 [2, 512, 1024], P(None, 'seq', 'rep')
- new_entries: bfloat16 [8, 512, 512], P('seq', None, 'rep')
Inputs may be any that keep to these rules, and one draw needn't show every extreme that they name: A request's cache holds its first cache_lengths entries; the most, 8192, is reached in every draw. `append_counts`: some request fills all 512 positions in every draw.
All inputs are finite; a program needn't handle non-finite values.
Results may differ from a plain program's by a relative error of at most 0.012.
The roundings to bfloat16 on the way count: a program that leaves them out, or rounds other values in their place, can miss the bound.
Values may be sent and summed in bfloat16 or wider, within the bound.
A program may use at most 64 MiB of HBM per device.

v0:
```python
import jax
import jax.numpy as jnp
from jax import lax
from jax.sharding import PartitionSpec as P


def attend(queries, new_keys, new_values, cache_piece, cache_length, valid_count):
    head_size = queries.shape[1]
    score_scale = head_size ** (-0.5)
    row_count = queries.shape[0]
    contract_last = (((1,), (1,)), ((), ()))
    fresh_scores = (
        lax.dot_general(queries, new_keys, contract_last, preferred_element_type=jnp.float32)
        * score_scale
    )
    position_ids = jnp.arange(row_count, dtype=jnp.int32)
    allowed = (position_ids[None, :] <= position_ids[:, None]) & (
        position_ids[None, :] < valid_count
    )
    fresh_scores = jnp.where(allowed, fresh_scores, -jnp.inf)
    row_max = fresh_scores.max(axis=1)
    fresh_exp = jnp.exp(fresh_scores - row_max[:, None])
    denominator = fresh_exp.sum(axis=1)
    accumulated = jnp.dot(
        fresh_exp.astype(jnp.bfloat16), new_values, preferred_element_type=jnp.float32
    )
    block_size = min(512, cache_piece.shape[0])

    def visit_block(block_index, state_tuple):
        running_max, running_sum, running_acc = state_tuple
        cache_block = lax.dynamic_slice_in_dim(cache_piece, block_index * block_size, block_size, 0)
        block_scores = (
            lax.dot_general(
                queries,
                cache_block[:, :head_size],
                contract_last,
                preferred_element_type=jnp.float32,
            )
            * score_scale
        )
        slot_ids = block_index * block_size + jnp.arange(block_size, dtype=jnp.int32)
        block_scores = jnp.where(slot_ids[None, :] < cache_length, block_scores, -jnp.inf)
        newer_max = jnp.maximum(running_max, block_scores.max(axis=1))
        factor = jnp.exp(running_max - newer_max)
        block_exp = jnp.exp(block_scores - newer_max[:, None])
        gathered_values = jnp.dot(
            block_exp.astype(jnp.bfloat16),
            cache_block[:, head_size:],
            preferred_element_type=jnp.float32,
        )
        return (
            newer_max,
            running_sum * factor + block_exp.sum(axis=1),
            running_acc * factor[:, None] + gathered_values,
        )

    block_total = (cache_length + block_size - 1) // block_size
    row_max, denominator, accumulated = lax.fori_loop(
        0, block_total, visit_block, (row_max, denominator, accumulated)
    )
    return (accumulated / denominator[:, None]).astype(jnp.bfloat16)


def on_device(
    hidden,
    w_query,
    w_key,
    w_value,
    w_out,
    norm_gain,
    norm_bias,
    kv_cache,
    cache_lengths,
    append_counts,
):
    seq_count = lax.axis_size("seq")
    requests, positions, model_width = hidden.shape
    head_size = kv_cache.shape[2] // 2
    group_size = w_query.shape[1] // head_size
    append_len = positions * seq_count
    flat_tokens = hidden.reshape(requests * positions, model_width)

    def project(weight_part):
        return jnp.dot(flat_tokens, weight_part, preferred_element_type=jnp.float32).astype(
            jnp.bfloat16
        )

    stacked = jnp.stack([project(w_query), project(w_key), project(w_value)], axis=1)
    stacked = stacked.reshape(requests, positions, 3, group_size, head_size).transpose(
        0, 3, 2, 1, 4
    )
    outgoing = stacked.reshape(seq_count, 3, positions * head_size)
    incoming = lax.all_to_all(outgoing, "seq", split_axis=0, concat_axis=2, tiled=True)
    incoming = incoming.reshape(3, append_len, head_size)
    lane_number = lax.axis_index("seq")
    request_id = lane_number // group_size
    cache_length = cache_lengths[request_id]
    valid_count = append_counts[request_id]
    queries = incoming[0]
    new_keys = incoming[1]
    new_values = incoming[2]
    attended = attend(queries, new_keys, new_values, kv_cache[0], cache_length, valid_count)
    position_ids = jnp.arange(append_len, dtype=jnp.int32)
    appended = jnp.concatenate([new_keys, new_values], axis=1)
    appended = jnp.where((position_ids < valid_count)[:, None], appended, jnp.zeros_like(appended))[
        None
    ]
    returned = lax.all_to_all(
        attended.reshape(seq_count, positions * head_size),
        "seq",
        split_axis=0,
        concat_axis=0,
        tiled=True,
    )
    heads_local = returned.reshape(requests, group_size, positions, head_size).transpose(0, 2, 1, 3)
    heads_local = heads_local.reshape(requests * positions, group_size * head_size)
    partial_out = jnp.dot(heads_local, w_out, preferred_element_type=jnp.float32)
    rep_index = lax.axis_index("rep")
    share_width = norm_gain.shape[0]
    summed = lax.psum(partial_out.astype(jnp.bfloat16), "rep").astype(jnp.float32)
    combined = flat_tokens.astype(jnp.float32) + summed
    mean_row = combined.sum(axis=1) / model_width
    square_row = (combined * combined).sum(axis=1) / model_width
    combined = lax.dynamic_slice_in_dim(combined, rep_index * share_width, share_width, 1)
    variance = square_row - mean_row * mean_row
    normed = (combined - mean_row[:, None]) * lax.rsqrt(variance + 1e-05)[
        :, None
    ] * norm_gain + norm_bias
    return (normed.astype(jnp.bfloat16).reshape(requests, positions, share_width), appended)


def solution(mesh):
    return jax.shard_map(
        on_device,
        mesh=mesh,
        in_specs=(
            P(None, "seq", None),
            P(None, "rep"),
            P(None, "rep"),
            P(None, "rep"),
            P("rep", None),
            P("rep"),
            P("rep"),
            P("seq", None, "rep"),
            P(),
            P(),
        ),
        out_specs=(P(None, "seq", "rep"), P("seq", None, "rep")),
        check_vma=False,
    )
```

profile of v0, /device:TPU:0, one launch (start us, length us, event | category | flops | bytes accessed | tf_op | source)
XLA Modules:
  0.0 138.0 jit_solution(14946720684066936791)
XLA Ops:
  7.2 1.5 %convolution_convert_fusion.3 = bf16[128,256]{1,0:T(8,128)(2,1)S(1)} fusion(bf16[128,1024]{1,0:T(8,128)(2,1)} %bitcast.34, bf16[1024,256]{1,0:T(8,128)(2,1)} %param.13), kind=kOutput, calls=%fused_computation.18 | convolution fusion | flops 67141632 | bytes 851968 | tf_op jit(solution)/shard_map/dot_general | solution.py:84
  8.8 1.4 convolution_convert_fusion.2
  10.4 0.2 convolution_convert_fusion.1
  10.9 0.4 reshape.123
  11.2 0.9 copy.20
  12.1 7.3 %all-to-all-start = ((bf16[8,3,4096]{2,1,0:T(4,128)(2,1)}), bf16[8,3,4096]{2,1,0:T(4,128)(2,1)S(1)}, u32[]{:S(2)}, u32[]{:S(2)}) async-start(bf16[8,3,4096]{2,1,0:T(4,128)(2,1)} %copy.20), calls=%async_computation | async-start | bytes 524288 | tf_op jit(solution)/shard_map/all_to_all | solution.py:93
  19.4 0.6 dynamic_slice.13
  20.6 0.6 dynamic_slice.12
  21.2 0.6 iota_compare_fusion.1
  21.9 6.4 %all-to-all-done = bf16[8,3,4096]{2,1,0:T(4,128)(2,1)S(1)} async-done(((bf16[8,3,4096]{2,1,0:T(4,128)(2,1)}), bf16[8,3,4096]{2,1,0:T(4,128)(2,1)S(1)}, u32[]{:S(2)}, u32[]{:S(2)}) %all-to-all-start) | async-done | bytes 196640 | tf_op jit(solution)/shard_map/all_to_all | solution.py:93
  28.3 0.8 slice_reduce_fusion
  29.3 0.2 squeeze.21
  29.4 0.2 squeeze.20
  29.6 0.3 fusion.17
  30.0 0.2 fusion.11
  30.2 0.3 fusion.12
  30.5 3.4 %while.14 = (s32[]{:T(128)}, f32[512]{0:T(512)S(1)}, f32[512]{0:T(512)S(1)}, f32[512,64]{0,1:T(8,128)S(1)}, s32[]{:T(128)}, /*index=5*/s32[]{:T(128)}, bf16[8704...) while((s32[]{:T(128)}, f32[512]{0:T(512)S(1)}, ...), condition=%wide.region_5.6_spmd, body=%wide.region_2.5_spmd.sunk | while | flops 69011456 | bytes 3769547 | solution.py:58
  30.5 0.6 add_compare_fusion.2
  31.1 1.2 fusion.38
  32.4 0.2 fusion.39
  32.6 1.3 convolution_add_fusion.2
  34.1 0.5 broadcast.94
  34.6 1.0 reduce.11
  35.7 0.7 reshape.133
  36.4 54.4 %all-to-all-start.1 = ((bf16[8,2,2048]{2,1,0:T(2,128)(2,1)}), bf16[8,2,2048]{2,1,0:T(2,128)(2,1)S(1)}, u32[]{:S(2)}, u32[]{:S(2)}) async-start(bf16[8,2,2048]{2,1,0:T(2,128)(2,1)} %reshape.133), calls=%async_computation.1 | async-start | bytes 131072 | tf_op jit(solution)/shard_map/all_to_all | solution.py:108
  91.2 6.5 %all-to-all-done.1 = bf16[8,2,2048]{2,1,0:T(2,128)(2,1)S(1)} async-done(((bf16[8,2,2048]{2,1,0:T(2,128)(2,1)}), bf16[8,2,2048]{2,1,0:T(2,128)(2,1)S(1)}, u32[]{:S(2)}, u32[]{:S(2)}) %all-to-all-start.1) | async-done | bytes 65568 | tf_op jit(solution)/shard_map/all_to_all | solution.py:108
  97.8 0.4 reduce.5
  98.6 0.9 convolution_convert_fusion
  99.5 0.8 maximum_select_fusion
  100.4 28.8 %all-reduce.2.cloned.1.call-done = bf16[128,1024]{1,0:T(8,128)(2,1)} async-done(((bf16[128,1024]{1,0:T(8,128)(2,1)}), bf16[128,1024]{1,0:T(8,128)(2,1)}) %all-reduce.2.cloned.1.call-update) | async-done | bytes 262160 | tf_op jit(solution)/shard_map/psum | solution.py:120
  129.2 1.1 fusion.15
  130.4 0.7 add_convert_fusion
  (37 shorter events, 1.9 us)
Async XLA Ops:
  7.2 91.4 %copy-start = (bf16[256,1024]{1,0:T(8,128)(2,1)S(1)}, bf16[256,1024]{1,0:T(8,128)(2,1)}, u32[]{:S(2)}) copy-start(bf16[256,1024]{1,0:T(8,128)(2,1)} %param.16) | copy-start | bytes 1572868
  7.2 3.2 %copy-start.1 = (bf16[2,64,1024]{2,1,0:T(8,128)(2,1)S(1)}, bf16[2,64,1024]{2,1,0:T(8,128)(2,1)}, u32[]{:S(2)}) copy-start(bf16[2,64,1024]{2,1,0:T(8,128)(2,1)} %param.12) | copy-start | bytes 786436
  7.2 3.2 %copy-start.2 = (bf16[1024,256]{1,0:T(8,128)(2,1)S(1)}, bf16[1024,256]{1,0:T(8,128)(2,1)}, u32[]{:S(2)}) copy-start(bf16[1024,256]{1,0:T(8,128)(2,1)} %param.15) | copy-start | bytes 1572868
  10.2 9.2 %copy-start.5 = (s32[2]{0:T(128)S(1)}, s32[2]{0:T(128)}, u32[]{:S(2)}) copy-start(s32[2]{0:T(128)} %param.20) | copy-start | bytes 28
  10.2 10.5 %copy-start.6 = (s32[2]{0:T(128)S(1)}, s32[2]{0:T(128)}, u32[]{:S(2)}) copy-start(s32[2]{0:T(128)} %param.21) | copy-start | bytes 28
  12.1 16.2 %all-to-all-start = ((bf16[8,3,4096]{2,1,0:T(4,128)(2,1)}), bf16[8,3,4096]{2,1,0:T(4,128)(2,1)S(1)}, u32[]{:S(2)}, u32[]{:S(2)}) async-start(bf16[8,3,4096]{2,1,0:T(4,128)(2,1)} %copy.20), calls=%async_computation | async-start | bytes 524288 | tf_op jit(solution)/shard_map/all_to_all | solution.py:93
  34.6 95.7 %copy-start.3 = (f32[256]{0:T(256)S(1)}, f32[256]{0:T(256)}, u32[]{:S(2)}) copy-start(f32[256]{0:T(256)} %param.18) | copy-start | bytes 3076
  34.6 95.7 %copy-start.4 = (f32[256]{0:T(256)S(1)}, f32[256]{0:T(256)}, u32[]{:S(2)}) copy-start(f32[256]{0:T(256)} %param.17) | copy-start | bytes 3076
  36.4 61.3 %all-to-all-start.1 = ((bf16[8,2,2048]{2,1,0:T(2,128)(2,1)}), bf16[8,2,2048]{2,1,0:T(2,128)(2,1)S(1)}, u32[]{:S(2)}, u32[]{:S(2)}) async-start(bf16[8,2,2048]{2,1,0:T(2,128)(2,1)} %reshape.133), calls=%async_computation.1 | async-start | bytes 131072 | tf_op jit(solution)/shard_map/all_to_all | solution.py:108
  90.8 38.4 %all-reduce.2.cloned.1.call-start = ((), (), s32[]{:S(2)}) async-start(), calls=%async_computation.2 | async-start | bytes 524288 | tf_op jit(solution)/shard_map/psum | solution.py:120
Sparse Core Ops, SparseCore 0:
  99.7 29.5 all-reduce.1
where the time goes:
time: 139 us; the launch traced here: 138 us
  starting transfers between devices  61.7 us (44%)
  waiting for transfers between devices  41.7 us (30%)
  between operations  14.9 us (11%)
  matrix products  7.1 us (5%)
  local copies, waits for them, and re-layouts  6.5 us (5%)
  other arithmetic  5.93 us (4%)
    all_to_all x1, starting transfers between devices, on_device(): lax.all_to_all(attended.reshape(seq_count, positions * head_size), 'seq',...  54.4 us
    psum x1, waiting for transfers between devices, on_device(): lax.psum(partial_out.astype(jnp.bfloat16), 'rep').astype(jnp.float32)  28.8 us
    all_to_all x1, starting transfers between devices, on_device(): lax.all_to_all(outgoing, 'seq', split_axis=0, concat_axis=2, tiled=True)  7.25 us
    all_to_all x1, waiting for transfers between devices, on_device(): lax.all_to_all(attended.reshape(seq_count, positions * head_size), 'seq',...  6.49 us
    all_to_all x1, waiting for transfers between devices, on_device(): lax.all_to_all(outgoing, 'seq', split_axis=0, concat_axis=2, tiled=True)  6.37 us
    dot_general x3, matrix products, project(): jnp.dot(flat_tokens, weight_part, preferred_element_type=jnp.float32)  3.04 us
  transfers between devices with their start and end apart: 3, of which 3 were waited for; matrix products, arithmetic and copies ran while one was open for 2% of the time, Pallas kernels for 0%

commit v1 on v0

--- a/solution.py
+++ b/solution.py
@@ -1,6 +1,10 @@
+import functools
+
 import jax
 import jax.numpy as jnp
 from jax import lax
+from jax.experimental import pallas as pl
+from jax.experimental.pallas import tpu as pltpu
 from jax.sharding import PartitionSpec as P
 
 
@@ -129,9 +133,393 @@
     return (normed.astype(jnp.bfloat16).reshape(requests, positions, share_width), appended)
 
 
+MESH = pl.DeviceIdType.MESH
+NEG = -1e30
+KEY_ROWS = 1024
+QUERY_ROWS = 128
+
+
+def fused_kernel(
+    seq_count,
+    lengths_ref,
+    counts_ref,
+    hidden_hbm,
+    wq_hbm,
+    wk_hbm,
+    wv_hbm,
+    wo_hbm,
+    gain_ref,
+    bias_ref,
+    kv_hbm,
+    out_ref,
+    entries_ref,
+    hid,
+    wq,
+    wk,
+    wv,
+    wo,
+    keys,
+    values,
+    scores,
+    q_send,
+    q_recv,
+    kv_send,
+    kv_recv,
+    queries,
+    new_values,
+    ret_send,
+    ret,
+    heads,
+    z_all,
+    load_sem,
+    q_ss,
+    q_rs,
+    kv_ss,
+    kv_rs,
+    wo_ss,
+    wo_rs,
+    ret_ss,
+    ret_rs,
+    pair_ss,
+    pair_rs,
+):
+    bf16, f32 = jnp.bfloat16, jnp.float32
+    lane = lax.axis_index("seq")
+    rep = lax.axis_index("rep")
+    far = lax.rem(rep + 2, 4)
+    pair = rep + 1 - 2 * lax.rem(rep, 2)
+    positions = hid.shape[0] // 2
+    half = positions // 2
+    width = hid.shape[1]
+    share = wq.shape[1]
+    append_len = queries.shape[0]
+    cached = keys.shape[0]
+    contract_last = (((1,), (1,)), ((), ()))
+
+    def remote(src, dst, send, recv, to_seq, to_rep):
+        return pltpu.make_async_remote_copy(
+            src_ref=src,
+            dst_ref=dst,
+            send_sem=send,
+            recv_sem=recv,
+            device_id=(to_seq, to_rep),
+            device_id_type=MESH,
+        )
+
+    barrier = pltpu.get_barrier_semaphore()
+    for k in range(1, seq_count):
+        pl.semaphore_signal(
+            barrier, inc=1, device_id=(lax.rem(lane + k, seq_count), rep), device_id_type=MESH
+        )
+    for k in range(seq_count):
+        pl.semaphore_signal(
+            barrier, inc=1, device_id=(lax.rem(lane + k, seq_count), far), device_id_type=MESH
+        )
+    pl.semaphore_signal(barrier, inc=1, device_id=(lane, pair), device_id_type=MESH)
+
+    loads = [
+        pltpu.make_async_copy(hidden_hbm, hid, load_sem.at[0]),
+        pltpu.make_async_copy(wq_hbm, wq, load_sem.at[1]),
+        pltpu.make_async_copy(wk_hbm, wk, load_sem.at[2]),
+        pltpu.make_async_copy(wv_hbm, wv, load_sem.at[3]),
+        pltpu.make_async_copy(kv_hbm.at[0, pl.ds(0, cached)], keys, load_sem.at[4]),
+        pltpu.make_async_copy(wo_hbm, wo.at[rep], load_sem.at[5]),
+    ]
+    for copy in loads:
+        copy.start()
+
+    loads[0].wait()
+    loads[1].wait()
+    q_all = jnp.dot(hid[...], wq[...], preferred_element_type=f32).astype(bf16).astype(f32)
+    q_all = q_all * 0.125
+    for dest in range(seq_count):
+        r, i = dest // 4, dest % 4
+        top = q_all[r * positions : r * positions + half, i * 64 : (i + 1) * 64]
+        low = q_all[r * positions + half : (r + 1) * positions, i * 64 : (i + 1) * 64]
+        q_send[dest] = jnp.concatenate([top, low], axis=1).astype(bf16)
+    pl.semaphore_wait(barrier, 2 * seq_count)
+
+    def q_copy(k):
+        to = lax.rem(lane + k, seq_count)
+        return remote(q_send.at[to], q_recv.at[lane], q_ss.at[k], q_rs.at[k], to, rep)
+
+    for k in range(1, seq_count):
+        q_copy(k).start()
+    q_recv[lane] = q_send[lane]
+
+    loads[2].wait()
+    loads[3].wait()
+    k_all = jnp.dot(hid[...], wk[...], preferred_element_type=f32)
+    v_all = jnp.dot(hid[...], wv[...], preferred_element_type=f32)
+    for dest in range(seq_count):
+        r, i = dest // 4, dest % 4
+        rows = slice(r * positions, (r + 1) * positions)
+        cols = slice(i * 64, (i + 1) * 64)
+        kv_send[dest] = jnp.concatenate([k_all[rows, cols], v_all[rows, cols]], axis=1).astype(bf16)
+
+    def kv_copy(k):
+        to = lax.rem(lane + k, seq_count)
+        return remote(
+            kv_send.at[to],
+            kv_recv.at[lane],
+            kv_ss.at[k],
+            kv_rs.at[k],
+            to,
+            rep,
+        )
+
+    for k in range(1, seq_count):
+        kv_copy(k).start()
+    kv_recv[lane] = kv_send[lane]
+
+    loads[5].wait()
+    wo_far = remote(wo.at[rep], wo.at[rep], wo_ss.at[0], wo_rs.at[0], lane, far)
+    wo_pair = remote(wo.at[rep], wo.at[rep], wo_ss.at[1], wo_rs.at[1], lane, pair)
+    wo_pass = remote(wo.at[far], wo.at[far], wo_ss.at[2], wo_rs.at[2], lane, pair)
+    wo_far.start()
+    wo_pair.start()
+
+    request = lane // 4
+    length = lengths_ref[request]
+    count = counts_ref[request]
+    loads[4].wait()
+    first = keys[0:16, :].astype(f32)[0:1, :]
+    mask_rows = 256
+    lanes = lax.broadcasted_iota(jnp.int32, (mask_rows, 128), 1)
+    row_ids = lax.broadcasted_iota(jnp.int32, (mask_rows, 128), 0)
+
+    def mask_block(b, carry):
+        rows = pl.ds(pl.multiple_of(b * mask_rows, mask_rows), mask_rows)
+        block = keys[rows, :].astype(f32)
+        keep = row_ids + b * mask_rows < length
+        keys[rows, :] = jnp.where(keep, block, first).astype(bf16)
+        values[rows, :] = jnp.where(keep, jnp.where(lanes < 64, 1.0, block), 0.0).astype(bf16)
+        return carry
+
+    lax.fori_loop(0, cached // mask_rows, mask_block, 0)
+
+    for k in range(1, seq_count):
+        q_copy(k).wait_recv()
+    lane_half = lax.broadcasted_iota(jnp.int32, (half, 128), 1) < 64
+    for s in range(seq_count):
+        both = q_recv[s].astype(f32)
+        queries[s * positions : s * positions + half, :] = jnp.where(lane_half, both, 0.0).astype(bf16)
+        queries[s * positions + half : (s + 1) * positions, :] = jnp.where(
+            lane_half, pltpu.roll(both, 64, 1), 0.0
+        ).astype(bf16)
+
+    chunks = append_len // QUERY_ROWS
+    per_chunk = QUERY_ROWS // positions
+    own_chunk = lane // per_chunk
+
+    for k in range(1, seq_count):
+        kv_copy(k).wait_recv()
+    lane_new = lax.broadcasted_iota(jnp.int32, (positions, 128), 1) < 64
+    row_new = lax.broadcasted_iota(jnp.int32, (positions, 128), 0)
+    for s in range(seq_count):
+        block = kv_recv[s].astype(f32)
+        new_values[s * positions : (s + 1) * positions, :] = jnp.where(lane_new, 1.0, block).astype(
+            bf16
+        )
+        entries_ref[s * positions : (s + 1) * positions, :] = jnp.where(
+            row_new + s * positions < count, block, 0.0
+        ).astype(bf16)
+
+    def ret_copy(side, s):
+        to_rep = rep if side == 0 else far
+        return remote(
+            ret_send.at[s], ret.at[rep, lane], ret_ss.at[side, s], ret_rs.at[side, lane], s, to_rep
+        )
+
+    def visit_chunk(step, carry):
+        chunk = lax.rem(own_chunk + 1 + step, chunks)
+        start = pl.multiple_of(chunk * QUERY_ROWS, QUERY_ROWS)
+        q = queries[pl.ds(start, QUERY_ROWS), :]
+        fresh = lax.dot_general(
+            q,
+            kv_recv[...].reshape(append_len, 128),
+            contract_last,
+            preferred_element_type=f32,
+        )
+        col = lax.broadcasted_iota(jnp.int32, (QUERY_ROWS, append_len), 1)
+        row = lax.broadcasted_iota(jnp.int32, (QUERY_ROWS, append_len), 0) + start
+        fresh = jnp.where((col <= row) & (col < count), fresh, NEG)
+        top = fresh.max(axis=1, keepdims=True)
+        for b in range(cached // KEY_ROWS):
+            rows = slice(b * KEY_ROWS, (b + 1) * KEY_ROWS)
+            block = lax.dot_general(q, keys[rows, :], contract_last, preferred_element_type=f32)
+            scores[:, rows] = block
+            top = jnp.maximum(top, block.max(axis=1, keepdims=True))
+        total = jnp.dot(
+            jnp.exp(fresh - top).astype(bf16), new_values[...], preferred_element_type=f32
+        )
+        for b in range(cached // KEY_ROWS):
+            rows = slice(b * KEY_ROWS, (b + 1) * KEY_ROWS)
+            weight = jnp.exp(scores[:, rows] - top).astype(bf16)
+            total = total + jnp.dot(weight, values[rows, :], preferred_element_type=f32)
+        attn = total / pltpu.roll(total, 64, 1)
+        for t in range(per_chunk):
+            a = attn[t * positions : t * positions + half, :]
+            b = attn[t * positions + half : (t + 1) * positions, :]
+            s = chunk * per_chunk + t
+            ret_send[s] = jnp.where(lane_half, pltpu.roll(a, 64, 1), b).astype(bf16)
+            ret_copy(1, s).start()
+
+            @pl.when(s != lane)
+            def _():
+                ret_copy(0, s).start()
+
+            @pl.when(s == lane)
+            def _():
+                ret[rep, lane] = ret_send[s]
+
+        return carry
+
+    lax.fori_loop(0, chunks, visit_chunk, 0)
+
+    wo_far.wait_recv()
+    wo_pass.start()
+
+    for k in range(seq_count):
+        s = lax.rem(lane + k, seq_count)
+        remote(
+            ret_send.at[s], ret.at[far, s], ret_ss.at[1, s], ret_rs.at[1, s], s, far
+        ).wait_recv()
+    far_pair = remote(ret.at[far], ret.at[far], pair_ss.at[1], pair_rs.at[1], lane, pair)
+    far_pair.start()
+    for k in range(1, seq_count):
+        s = lax.rem(lane + k, seq_count)
+        remote(
+            ret_send.at[s], ret.at[rep, s], ret_ss.at[0, s], ret_rs.at[0, s], s, rep
+        ).wait_recv()
+    own_pair = remote(ret.at[rep], ret.at[rep], pair_ss.at[0], pair_rs.at[0], lane, pair)
+    own_pair.start()
+
+    def project(which):
+        for r in range(2):
+            parts = [ret[which, r * 4 + i].astype(f32) for i in range(4)]
+            upper = [jnp.where(lane_half, parts[2 * g], pltpu.roll(parts[2 * g + 1], 64, 1)) for g in range(2)]
+            lower = [jnp.where(lane_half, pltpu.roll(parts[2 * g], 64, 1), parts[2 * g + 1]) for g in range(2)]
+            for g in range(2):
+                cols = slice(g * 128, (g + 1) * 128)
+                heads[r * positions : r * positions + half, cols] = upper[g].astype(bf16)
+                heads[r * positions + half : (r + 1) * positions, cols] = lower[g].astype(bf16)
+        part = jnp.dot(heads[...], wo[which], preferred_element_type=f32)
+        return part.astype(bf16).astype(f32)
+
+    z_all[...] = hid[...].astype(f32) + project(rep)
+    z_all[...] += project(far)
+    wo_pair.wait_recv()
+    wo_pass.wait_recv()
+    own_pair.wait_recv()
+    z_all[...] += project(pair)
+    far_pair.wait_recv()
+    z_all[...] += project(lax.rem(pair + 2, 4))
+    z = z_all[...]
+    mean = z.sum(axis=1, keepdims=True) / width
+    square = (z * z).sum(axis=1, keepdims=True) / width
+    mine = z_all[:, pl.ds(pl.multiple_of(rep * share, share), share)]
+    scale = lax.rsqrt(square - mean * mean + 1e-05)
+    out_ref[...] = ((mine - mean) * scale * gain_ref[...] + bias_ref[...]).astype(bf16)
+
+    for k in range(1, seq_count):
+        q_copy(k).wait_send()
+        kv_copy(k).wait_send()
+    for k in range(seq_count):
+        s = lax.rem(lane + k, seq_count)
+        ret_copy(1, s).wait_send()
+        if k:
+            ret_copy(0, s).wait_send()
+    for copy in (wo_far, wo_pair, wo_pass, own_pair, far_pair):
+        copy.wait_send()
+
+
+def fused(
+    hidden,
+    w_query,
+    w_key,
+    w_value,
+    w_out,
+    norm_gain,
+    norm_bias,
+    kv_cache,
+    cache_lengths,
+    append_counts,
+):
+    seq_count = lax.axis_size("seq")
+    requests, positions, width = hidden.shape
+    share = w_query.shape[1]
+    tokens = requests * positions
+    append_len = positions * seq_count
+    cached = kv_cache.shape[1] - append_len
+    bf16, f32 = jnp.bfloat16, jnp.float32
+    any_spec = pl.BlockSpec(memory_space=pl.ANY)
+    vmem_spec = pl.BlockSpec(memory_space=pltpu.VMEM)
+    smem_spec = pl.BlockSpec(memory_space=pltpu.SMEM)
+    dma = pltpu.SemaphoreType.DMA
+    half = positions // 2
+    out, entries = pl.pallas_call(
+        functools.partial(fused_kernel, seq_count),
+        out_shape=(
+            jax.ShapeDtypeStruct((tokens, share), bf16),
+            jax.ShapeDtypeStruct((append_len, 128), bf16),
+        ),
+        in_specs=[smem_spec] * 2 + [any_spec] * 5 + [vmem_spec] * 2 + [any_spec],
+        out_specs=(vmem_spec, vmem_spec),
+        scratch_shapes=[
+            pltpu.VMEM((tokens, width), bf16),
+            pltpu.VMEM((width, share), bf16),
+            pltpu.VMEM((width, share), bf16),
+            pltpu.VMEM((width, share), bf16),
+            pltpu.VMEM((4, share, width), bf16),
+            pltpu.VMEM((cached, 128), bf16),
+            pltpu.VMEM((cached, 128), bf16),
+            pltpu.VMEM((QUERY_ROWS, cached), f32),
+            pltpu.VMEM((seq_count, half, 128), bf16),
+            pltpu.VMEM((seq_count, half, 128), bf16),
+            pltpu.VMEM((seq_count, positions, 128), bf16),
+            pltpu.VMEM((seq_count, positions, 128), bf16),
+            pltpu.VMEM((append_len, 128), bf16),
+            pltpu.VMEM((append_len, 128), bf16),
+            pltpu.VMEM((seq_count, half, 128), bf16),
+            pltpu.VMEM((4, seq_count, half, 128), bf16),
+            pltpu.VMEM((tokens, share), bf16),
+            pltpu.VMEM((tokens, width), f32),
+            dma((6,)),
+            dma((seq_count,)),
+            dma((seq_count,)),
+            dma((seq_count,)),
+            dma((seq_count,)),
+            dma((3,)),
+            dma((3,)),
+            dma((2, seq_count)),
+            dma((2, seq_count)),
+            dma((2,)),
+            dma((2,)),
+        ],
+        compiler_params=pltpu.CompilerParams(
+            collective_id=0, has_side_effects=True, vmem_limit_bytes=40 * 1024 * 1024
+        ),
+        name="sublayer",
+    )(
+        cache_lengths,
+        append_counts,
+        hidden.reshape(tokens, width),
+        w_query,
+        w_key,
+        w_value,
+        w_out,
+        norm_gain.reshape(1, share),
+        norm_bias.reshape(1, share),
+        kv_cache,
+    )
+    return out.reshape(requests, positions, share), entries[None]
+
+
 def solution(mesh):
+    fits = mesh.shape["seq"] == 8 and mesh.shape["rep"] == 4
     return jax.shard_map(
-        on_device,
+        fused if fits else on_device,
         mesh=mesh,
         in_specs=(
             P(None, "seq", None),

time: 139 us -> 38.8 us (0.28)
  the two profiles are of different devices: /device:TPU:0 before, /device:TPU:1 now
where the time goes in v1:
time: 38.8 us; the launch traced here: 38.4 us
  Pallas kernels  27 us (70%)
  local copies, waits for them, and re-layouts  10.7 us (28%)
  between operations  0.66 us (2%)
    pallas_call x1, Pallas kernels, fused(): pl.pallas_call(functools.partial(fused_kernel, seq_count), out_shape=(jax...  27 us
    unnamed x22, local copies, waits for them, and re-layouts  10.7 us

profile of v1, /device:TPU:1, one launch (start us, length us, event | category | flops | bytes accessed | tf_op | source)
XLA Modules:
  0.0 38.4 jit_solution(2582235451447720169)
XLA Ops:
  0.6 0.0 copy-start
  0.6 1.6 %copy-done = bf16[1,8704,128]{2,1,0:T(8,128)(2,1)S(1)} copy-done((bf16[1,8704,128]{2,1,0:T(8,128)(2,1)S(1)}, bf16[1,8704,128]{2,1,0:T(8,128)(2,1)}, u32[]{:S(2)}) %copy-start) | copy-done | bytes 2228248
  2.3 0.0 copy-start.1
  2.3 1.0 %copy-done.1 = bf16[1024,256]{1,0:T(8,128)(2,1)S(1)} copy-done((bf16[1024,256]{1,0:T(8,128)(2,1)S(1)}, bf16[1024,256]{1,0:T(8,128)(2,1)}, u32[]{:S(2)}) %copy-start.1) | copy-done | bytes 524312
  3.3 0.0 copy-start.2
  3.3 1.0 %copy-done.2 = bf16[1024,256]{1,0:T(8,128)(2,1)S(1)} copy-done((bf16[1024,256]{1,0:T(8,128)(2,1)S(1)}, bf16[1024,256]{1,0:T(8,128)(2,1)}, u32[]{:S(2)}) %copy-start.2) | copy-done | bytes 524312
  4.3 0.0 copy-start.3
  4.3 1.0 %copy-done.3 = bf16[1024,256]{1,0:T(8,128)(2,1)S(1)} copy-done((bf16[1024,256]{1,0:T(8,128)(2,1)S(1)}, bf16[1024,256]{1,0:T(8,128)(2,1)}, u32[]{:S(2)}) %copy-start.3) | copy-done | bytes 524312
  5.4 0.0 copy-start.4
  5.4 1.0 %copy-done.4 = bf16[256,1024]{1,0:T(8,128)(2,1)S(1)} copy-done((bf16[256,1024]{1,0:T(8,128)(2,1)S(1)}, bf16[256,1024]{1,0:T(8,128)(2,1)}, u32[]{:S(2)}) %copy-start.4) | copy-done | bytes 524312
  6.4 0.0 copy-start.5
  6.4 0.9 %copy-done.5 = bf16[2,64,1024]{2,1,0:T(8,128)(2,1)S(1)} copy-done((bf16[2,64,1024]{2,1,0:T(8,128)(2,1)S(1)}, bf16[2,64,1024]{2,1,0:T(8,128)(2,1)}, u32[]{:S(2)}) %copy-start.5) | copy-done | bytes 262168
  7.4 0.0 copy-start.6
  7.4 0.7 %copy-done.6 = f32[256]{0:T(256)S(1)} copy-done((f32[256]{0:T(256)S(1)}, f32[256]{0:T(256)}, u32[]{:S(2)}) %copy-start.6) | copy-done | bytes 1048
  8.1 0.0 copy-start.7
  8.1 0.7 %copy-done.7 = f32[256]{0:T(256)S(1)} copy-done((f32[256]{0:T(256)S(1)}, f32[256]{0:T(256)}, u32[]{:S(2)}) %copy-start.7) | copy-done | bytes 1048
  8.7 0.0 copy-start.8
  8.7 0.7 %copy-done.8 = s32[2]{0:T(128)S(1)} copy-done((s32[2]{0:T(128)S(1)}, s32[2]{0:T(128)}, u32[]{:S(2)}) %copy-start.8) | copy-done | bytes 32
  9.4 0.0 copy-start.9
  9.4 0.7 %copy-done.9 = s32[2]{0:T(128)S(1)} copy-done((s32[2]{0:T(128)S(1)}, s32[2]{0:T(128)}, u32[]{:S(2)}) %copy-start.9) | copy-done | bytes 32
  10.1 27.0 %sublayer.1 = (bf16[128,256]{1,0:T(8,128)(2,1)S(1)}, bf16[512,128]{1,0:T(8,128)(2,1)S(1)}) custom-call(s32[2]{0:T(128)S(1)} %copy-done.8, s32[2]{0:T(128)S(1)} %copy-done.9, bf16[128,1024]{1,0:T(8,128)(2,1)S(1)} %bitcast.5, bf16[1024,256]{1,0:T(8,128)(2,1)S(1)} %copy-done.1, bf16[1024,256]{1,0:T(8,128)(2,1)S(1)} %copy-done.2, ...), custom_call_target="tpu_custom_call" | custom-call | tf_op jit(solution)/shard_map/sublayer/pallas_call | solution.py:461
  37.1 0.6 %copy.14 = bf16[2,64,256]{2,1,0:T(8,128)(2,1)} copy(bf16[2,64,256]{2,1,0:T(8,128)(2,1)S(1)} %bitcast.7) | data formatting | bytes 131072
  37.7 0.7 %copy.15 = bf16[1,512,128]{2,1,0:T(8,128)(2,1)} copy(bf16[1,512,128]{2,1,0:T(8,128)(2,1)S(1)} %bitcast.6) | data formatting | bytes 262144
Async XLA Ops:
  0.6 1.6 %copy-start = (bf16[1,8704,128]{2,1,0:T(8,128)(2,1)S(1)}, bf16[1,8704,128]{2,1,0:T(8,128)(2,1)}, u32[]{:S(2)}) copy-start(bf16[1,8704,128]{2,1,0:T(8,128)(2,1)} %kv_hbm.1) | copy-start | bytes 6684676
  2.3 1.0 %copy-start.1 = (bf16[1024,256]{1,0:T(8,128)(2,1)S(1)}, bf16[1024,256]{1,0:T(8,128)(2,1)}, u32[]{:S(2)}) copy-start(bf16[1024,256]{1,0:T(8,128)(2,1)} %wq_hbm.1) | copy-start | bytes 1572868
  3.3 1.0 %copy-start.2 = (bf16[1024,256]{1,0:T(8,128)(2,1)S(1)}, bf16[1024,256]{1,0:T(8,128)(2,1)}, u32[]{:S(2)}) copy-start(bf16[1024,256]{1,0:T(8,128)(2,1)} %wk_hbm.1) | copy-start | bytes 1572868
  4.3 1.0 %copy-start.3 = (bf16[1024,256]{1,0:T(8,128)(2,1)S(1)}, bf16[1024,256]{1,0:T(8,128)(2,1)}, u32[]{:S(2)}) copy-start(bf16[1024,256]{1,0:T(8,128)(2,1)} %wv_hbm.1) | copy-start | bytes 1572868
  5.4 1.0 %copy-start.4 = (bf16[256,1024]{1,0:T(8,128)(2,1)S(1)}, bf16[256,1024]{1,0:T(8,128)(2,1)}, u32[]{:S(2)}) copy-start(bf16[256,1024]{1,0:T(8,128)(2,1)} %wo_hbm.1) | copy-start | bytes 1572868
  6.4 0.9 %copy-start.5 = (bf16[2,64,1024]{2,1,0:T(8,128)(2,1)S(1)}, bf16[2,64,1024]{2,1,0:T(8,128)(2,1)}, u32[]{:S(2)}) copy-start(bf16[2,64,1024]{2,1,0:T(8,128)(2,1)} %param.10) | copy-start | bytes 786436
  7.4 0.7 %copy-start.6 = (f32[256]{0:T(256)S(1)}, f32[256]{0:T(256)}, u32[]{:S(2)}) copy-start(f32[256]{0:T(256)} %param.15) | copy-start | bytes 3076
  8.1 0.7 %copy-start.7 = (f32[256]{0:T(256)S(1)}, f32[256]{0:T(256)}, u32[]{:S(2)}) copy-start(f32[256]{0:T(256)} %param.16) | copy-start | bytes 3076
  8.7 0.7 %copy-start.8 = (s32[2]{0:T(128)S(1)}, s32[2]{0:T(128)}, u32[]{:S(2)}) copy-start(s32[2]{0:T(128)} %lengths_ref.1) | copy-start | bytes 28
  9.4 0.7 %copy-start.9 = (s32[2]{0:T(128)S(1)}, s32[2]{0:T(128)}, u32[]{:S(2)}) copy-start(s32[2]{0:T(128)} %counts_ref.1) | copy-start | bytes 28

commit v2 on v1

--- a/solution.py
+++ b/solution.py
@@ -136,7 +136,7 @@
 MESH = pl.DeviceIdType.MESH
 NEG = -1e30
 KEY_ROWS = 1024
-QUERY_ROWS = 128
+QUERY_ROWS = 256
 
 
 def fused_kernel(
@@ -160,7 +160,6 @@
     wo,
     keys,
     values,
-    scores,
     q_send,
     q_recv,
     kv_send,
@@ -188,6 +187,10 @@
     rep = lax.axis_index("rep")
     far = lax.rem(rep + 2, 4)
     pair = rep + 1 - 2 * lax.rem(rep, 2)
+    cross = lax.rem(pair + 2, 4)
+    near_lanes = seq_count // 2
+    near_base = lane // near_lanes * near_lanes
+    away_base = near_lanes - near_base
     positions = hid.shape[0] // 2
     half = positions // 2
     width = hid.shape[1]
@@ -205,17 +208,6 @@
             device_id=(to_seq, to_rep),
             device_id_type=MESH,
         )
-
-    barrier = pltpu.get_barrier_semaphore()
-    for k in range(1, seq_count):
-        pl.semaphore_signal(
-            barrier, inc=1, device_id=(lax.rem(lane + k, seq_count), rep), device_id_type=MESH
-        )
-    for k in range(seq_count):
-        pl.semaphore_signal(
-            barrier, inc=1, device_id=(lax.rem(lane + k, seq_count), far), device_id_type=MESH
-        )
-    pl.semaphore_signal(barrier, inc=1, device_id=(lane, pair), device_id_type=MESH)
 
     loads = [
         pltpu.make_async_copy(hidden_hbm, hid, load_sem.at[0]),
@@ -228,6 +220,30 @@
     for copy in loads:
         copy.start()
 
+    barrier = pltpu.get_barrier_semaphore()
+    for k in range(1, seq_count):
+        pl.semaphore_signal(
+            barrier, inc=1, device_id=(lax.rem(lane + k, seq_count), rep), device_id_type=MESH
+        )
+    for k in range(seq_count):
+        pl.semaphore_signal(
+            barrier, inc=1, device_id=(lax.rem(lane + k, seq_count), far), device_id_type=MESH
+        )
+    for k in range(near_lanes):
+        for to in (pair, cross):
+            pl.semaphore_signal(
+                barrier,
+                inc=1,
+                device_id=(near_base + lax.rem(lane + k, near_lanes), to),
+                device_id_type=MESH,
+            )
+
+    wo_far = remote(wo_hbm, wo.at[rep], wo_ss.at[0], wo_rs.at[0], lane, far)
+    wo_pair = remote(wo_hbm, wo.at[rep], wo_ss.at[1], wo_rs.at[1], lane, pair)
+    wo_pass = remote(wo.at[far], wo.at[far], wo_ss.at[2], wo_rs.at[2], lane, pair)
+    pl.semaphore_wait(barrier, 3 * seq_count - 1)
+    wo_far.start()
+
     loads[0].wait()
     loads[1].wait()
     q_all = jnp.dot(hid[...], wq[...], preferred_element_type=f32).astype(bf16).astype(f32)
@@ -237,7 +253,6 @@
         top = q_all[r * positions : r * positions + half, i * 64 : (i + 1) * 64]
         low = q_all[r * positions + half : (r + 1) * positions, i * 64 : (i + 1) * 64]
         q_send[dest] = jnp.concatenate([top, low], axis=1).astype(bf16)
-    pl.semaphore_wait(barrier, 2 * seq_count)
 
     def q_copy(k):
         to = lax.rem(lane + k, seq_count)
@@ -272,11 +287,6 @@
         kv_copy(k).start()
     kv_recv[lane] = kv_send[lane]
 
-    loads[5].wait()
-    wo_far = remote(wo.at[rep], wo.at[rep], wo_ss.at[0], wo_rs.at[0], lane, far)
-    wo_pair = remote(wo.at[rep], wo.at[rep], wo_ss.at[1], wo_rs.at[1], lane, pair)
-    wo_pass = remote(wo.at[far], wo.at[far], wo_ss.at[2], wo_rs.at[2], lane, pair)
-    wo_far.start()
     wo_pair.start()
 
     request = lane // 4
@@ -308,92 +318,107 @@
             lane_half, pltpu.roll(both, 64, 1), 0.0
         ).astype(bf16)
 
-    chunks = append_len // QUERY_ROWS
     per_chunk = QUERY_ROWS // positions
     own_chunk = lane // per_chunk
-
-    for k in range(1, seq_count):
-        kv_copy(k).wait_recv()
     lane_new = lax.broadcasted_iota(jnp.int32, (positions, 128), 1) < 64
     row_new = lax.broadcasted_iota(jnp.int32, (positions, 128), 0)
-    for s in range(seq_count):
-        block = kv_recv[s].astype(f32)
-        new_values[s * positions : (s + 1) * positions, :] = jnp.where(lane_new, 1.0, block).astype(
-            bf16
-        )
-        entries_ref[s * positions : (s + 1) * positions, :] = jnp.where(
-            row_new + s * positions < count, block, 0.0
-        ).astype(bf16)
+
+    def take_new_entries():
+        for k in range(1, seq_count):
+            kv_copy(k).wait_recv()
+        for s in range(seq_count):
+            block = kv_recv[s].astype(f32)
+            rows = slice(s * positions, (s + 1) * positions)
+            new_values[rows, :] = jnp.where(lane_new, 1.0, block).astype(bf16)
+            entries_ref[rows, :] = jnp.where(
+                row_new + s * positions < count, block, 0.0
+            ).astype(bf16)
+
+    to_reps = (rep, far, pair, cross)
 
     def ret_copy(side, s):
-        to_rep = rep if side == 0 else far
         return remote(
-            ret_send.at[s], ret.at[rep, lane], ret_ss.at[side, s], ret_rs.at[side, lane], s, to_rep
-        )
-
-    def visit_chunk(step, carry):
-        chunk = lax.rem(own_chunk + 1 + step, chunks)
+            ret_send.at[s],
+            ret.at[rep, lane],
+            ret_ss.at[side, s],
+            ret_rs.at[side, lane],
+            s,
+            to_reps[side],
+        )
+
+    def wait_ret(side, s):
+        remote(
+            ret_send.at[s],
+            ret.at[to_reps[side], s],
+            ret_ss.at[side, s],
+            ret_rs.at[side, s],
+            s,
+            to_reps[side],
+        ).wait_recv()
+
+    blocks = cached // KEY_ROWS
+    for step in range(2):
+        chunk = 1 - own_chunk if step == 0 else own_chunk
         start = pl.multiple_of(chunk * QUERY_ROWS, QUERY_ROWS)
         q = queries[pl.ds(start, QUERY_ROWS), :]
-        fresh = lax.dot_general(
-            q,
-            kv_recv[...].reshape(append_len, 128),
-            contract_last,
-            preferred_element_type=f32,
-        )
-        col = lax.broadcasted_iota(jnp.int32, (QUERY_ROWS, append_len), 1)
-        row = lax.broadcasted_iota(jnp.int32, (QUERY_ROWS, append_len), 0) + start
-        fresh = jnp.where((col <= row) & (col < count), fresh, NEG)
-        top = fresh.max(axis=1, keepdims=True)
-        for b in range(cached // KEY_ROWS):
-            rows = slice(b * KEY_ROWS, (b + 1) * KEY_ROWS)
-            block = lax.dot_general(q, keys[rows, :], contract_last, preferred_element_type=f32)
-            scores[:, rows] = block
-            top = jnp.maximum(top, block.max(axis=1, keepdims=True))
-        total = jnp.dot(
-            jnp.exp(fresh - top).astype(bf16), new_values[...], preferred_element_type=f32
-        )
-        for b in range(cached // KEY_ROWS):
-            rows = slice(b * KEY_ROWS, (b + 1) * KEY_ROWS)
-            weight = jnp.exp(scores[:, rows] - top).astype(bf16)
-            total = total + jnp.dot(weight, values[rows, :], preferred_element_type=f32)
+
+        def block_scores(b):
+            if b < blocks:
+                block = keys[b * KEY_ROWS : (b + 1) * KEY_ROWS, :]
+                return lax.dot_general(q, block, contract_last, preferred_element_type=f32)
+            fresh = kv_recv[...].reshape(append_len, 128)
+            fresh = lax.dot_general(q, fresh, contract_last, preferred_element_type=f32)
+            col = lax.broadcasted_iota(jnp.int32, (QUERY_ROWS, append_len), 1)
+            row = lax.broadcasted_iota(jnp.int32, (QUERY_ROWS, append_len), 0) + start
+            return jnp.where((col <= row) & (col < count), fresh, NEG)
+
+        current = block_scores(0)
+        top = total = None
+        for b in range(blocks + 1):
+            following = None
+            if b < blocks:
+                if step == 0 and b == blocks - 1:
+                    take_new_entries()
+                following = block_scores(b + 1)
+            newer = current.max(axis=1, keepdims=True)
+            if b > 0:
+                newer = jnp.maximum(top, newer)
+            weight = jnp.exp(current - newer).astype(bf16)
+            rows = values[b * KEY_ROWS : (b + 1) * KEY_ROWS, :] if b < blocks else new_values[...]
+            part = jnp.dot(weight, rows, preferred_element_type=f32)
+            total = part if b == 0 else total * jnp.exp(top - newer) + part
+            top, current = newer, following
         attn = total / pltpu.roll(total, 64, 1)
         for t in range(per_chunk):
-            a = attn[t * positions : t * positions + half, :]
-            b = attn[t * positions + half : (t + 1) * positions, :]
+            upper = attn[t * positions : t * positions + half, :]
+            lower = attn[t * positions + half : (t + 1) * positions, :]
             s = chunk * per_chunk + t
-            ret_send[s] = jnp.where(lane_half, pltpu.roll(a, 64, 1), b).astype(bf16)
-            ret_copy(1, s).start()
-
-            @pl.when(s != lane)
-            def _():
+            ret_send[s] = jnp.where(lane_half, pltpu.roll(upper, 64, 1), lower).astype(bf16)
+            if step == 0:
                 ret_copy(0, s).start()
-
-            @pl.when(s == lane)
-            def _():
-                ret[rep, lane] = ret_send[s]
-
-        return carry
-
-    lax.fori_loop(0, chunks, visit_chunk, 0)
+                ret_copy(1, s).start()
+        if step == 1:
+            for k in range(near_lanes):
+                s = near_base + lax.rem(lane + k, near_lanes)
+                for side in range(4):
+                    if k or side:
+                        ret_copy(side, s).start()
+            ret[rep, lane] = ret_send[lane]
 
     wo_far.wait_recv()
     wo_pass.start()
 
-    for k in range(seq_count):
-        s = lax.rem(lane + k, seq_count)
-        remote(
-            ret_send.at[s], ret.at[far, s], ret_ss.at[1, s], ret_rs.at[1, s], s, far
-        ).wait_recv()
-    far_pair = remote(ret.at[far], ret.at[far], pair_ss.at[1], pair_rs.at[1], lane, pair)
-    far_pair.start()
-    for k in range(1, seq_count):
-        s = lax.rem(lane + k, seq_count)
-        remote(
-            ret_send.at[s], ret.at[rep, s], ret_ss.at[0, s], ret_rs.at[0, s], s, rep
-        ).wait_recv()
-    own_pair = remote(ret.at[rep], ret.at[rep], pair_ss.at[0], pair_rs.at[0], lane, pair)
-    own_pair.start()
+    passes = []
+    for side in (0, 1):
+        for k in range(near_lanes):
+            wait_ret(side, away_base + k)
+        away = ret.at[to_reps[side], pl.ds(away_base, near_lanes)]
+        passes.append(remote(away, away, pair_ss.at[side], pair_rs.at[side], lane, pair))
+        passes[side].start()
+    for k in range(near_lanes):
+        for side in range(4):
+            if k or side:
+                wait_ret(side, near_base + lax.rem(lane + k, near_lanes))
 
     def project(which):
         for r in range(2):
@@ -407,14 +432,15 @@
         part = jnp.dot(heads[...], wo[which], preferred_element_type=f32)
         return part.astype(bf16).astype(f32)
 
+    loads[5].wait()
     z_all[...] = hid[...].astype(f32) + project(rep)
     z_all[...] += project(far)
     wo_pair.wait_recv()
+    passes[0].wait_recv()
+    z_all[...] += project(pair)
     wo_pass.wait_recv()
-    own_pair.wait_recv()
-    z_all[...] += project(pair)
-    far_pair.wait_recv()
-    z_all[...] += project(lax.rem(pair + 2, 4))
+    passes[1].wait_recv()
+    z_all[...] += project(cross)
     z = z_all[...]
     mean = z.sum(axis=1, keepdims=True) / width
     square = (z * z).sum(axis=1, keepdims=True) / width
@@ -425,12 +451,13 @@
     for k in range(1, seq_count):
         q_copy(k).wait_send()
         kv_copy(k).wait_send()
-    for k in range(seq_count):
-        s = lax.rem(lane + k, seq_count)
-        ret_copy(1, s).wait_send()
-        if k:
-            ret_copy(0, s).wait_send()
-    for copy in (wo_far, wo_pair, wo_pass, own_pair, far_pair):
+    for k in range(near_lanes):
+        for side in range(4):
+            if side < 2:
+                ret_copy(side, away_base + k).wait_send()
+            if k or side:
+                ret_copy(side, near_base + lax.rem(lane + k, near_lanes)).wait_send()
+    for copy in [wo_far, wo_pair, wo_pass] + passes:
         copy.wait_send()
 
 
@@ -453,7 +480,7 @@
     append_len = positions * seq_count
     cached = kv_cache.shape[1] - append_len
     bf16, f32 = jnp.bfloat16, jnp.float32
-    any_spec = pl.BlockSpec(memory_space=pl.ANY)
+    any_spec = pl.BlockSpec(memory_space=pltpu.HBM)
     vmem_spec = pl.BlockSpec(memory_space=pltpu.VMEM)
     smem_spec = pl.BlockSpec(memory_space=pltpu.SMEM)
     dma = pltpu.SemaphoreType.DMA
@@ -474,7 +501,6 @@
             pltpu.VMEM((4, share, width), bf16),
             pltpu.VMEM((cached, 128), bf16),
             pltpu.VMEM((cached, 128), bf16),
-            pltpu.VMEM((QUERY_ROWS, cached), f32),
             pltpu.VMEM((seq_count, half, 128), bf16),
             pltpu.VMEM((seq_count, half, 128), bf16),
             pltpu.VMEM((seq_count, positions, 128), bf16),
@@ -492,13 +518,13 @@
             dma((seq_count,)),
             dma((3,)),
             dma((3,)),
-            dma((2, seq_count)),
-            dma((2, seq_count)),
+            dma((4, seq_count)),
+            dma((4, seq_count)),
             dma((2,)),
             dma((2,)),
         ],
         compiler_params=pltpu.CompilerParams(
-            collective_id=0, has_side_effects=True, vmem_limit_bytes=40 * 1024 * 1024
+            collective_id=0, has_side_effects=True, vmem_limit_bytes=63 * 1024 * 1024
         ),
         name="sublayer",
     )(

time: 38.8 us -> 29.7 us (0.77)
  local copies, waits for them, and re-layouts: 10.7 us -> 3.04 us
  Pallas kernels: 27 us -> 25.8 us
    unnamed x22 -> x2, local copies, waits for them, and re-layouts: 10.7 us -> 3.04 us
    pallas_call x1, Pallas kernels: 27 us -> 25.8 us  [fused(): pl.pallas_call(functools.partial(fused_kernel, seq_count), out_shape=(jax...]
where the time goes in v2:
time: 29.7 us; the launch traced here: 29.5 us
  Pallas kernels  25.8 us (87%)
  local copies, waits for them, and re-layouts  3.04 us (10%)
  between operations  0.64 us (2%)
    pallas_call x1, Pallas kernels, fused(): pl.pallas_call(functools.partial(fused_kernel, seq_count), out_shape=(jax...  25.8 us
    unnamed x2, local copies, waits for them, and re-layouts  3.04 us

profile of v2, /device:TPU:1, one launch (start us, length us, event | category | flops | bytes accessed | tf_op | source)
XLA Modules:
  0.0 29.5 jit_solution(10523594026598081840)
XLA Ops:
  0.6 25.8 %sublayer.1 = (bf16[128,256]{1,0:T(8,128)(2,1)}, bf16[512,128]{1,0:T(8,128)(2,1)}) custom-call(s32[2]{0:T(128)} %lengths_ref.1, s32[2]{0:T(128)} %counts_ref.1, bf16[128,1024]{1,0:T(8,128)(2,1)} %bitcast.5, bf16[1024,256]{1,0:T(8,128)(2,1)} %wq_hbm.1, bf16[1024,256]{1,0:T(8,128)(2,1)} %wk_hbm.1, bf16[1024,256]{1,0:T(8,128)(2,1)} %wv_hbm.1, ...), custom_call_target="tpu_custom_call" | custom-call | tf_op jit(solution)/shard_map/sublayer/pallas_call | solution.py:488
  26.5 1.5 %copy.14 = bf16[2,64,256]{2,1,0:T(8,128)(2,1)} copy(bf16[2,64,256]{2,1,0:T(8,128)(2,1)} %bitcast.7) | data formatting | bytes 131072
  28.0 1.6 %copy.15 = bf16[1,512,128]{2,1,0:T(8,128)(2,1)} copy(bf16[1,512,128]{2,1,0:T(8,128)(2,1)} %bitcast.6) | data formatting | bytes 262144

commit v3 on v2

--- a/solution.py
+++ b/solution.py
@@ -238,11 +238,19 @@
                 device_id_type=MESH,
             )
 
-    wo_far = remote(wo_hbm, wo.at[rep], wo_ss.at[0], wo_rs.at[0], lane, far)
+    cut = share // 2
+    wo_far, wo_pass = [], []
+    for h in range(2):
+        rows = pl.ds(h * cut, cut)
+        wo_far.append(
+            remote(wo_hbm.at[rows], wo.at[rep, rows], wo_ss.at[2 * h], wo_rs.at[2 * h], lane, far)
+        )
+        held = wo.at[far, rows]
+        wo_pass.append(remote(held, held, wo_ss.at[2 * h + 3], wo_rs.at[2 * h + 3], lane, pair))
     wo_pair = remote(wo_hbm, wo.at[rep], wo_ss.at[1], wo_rs.at[1], lane, pair)
-    wo_pass = remote(wo.at[far], wo.at[far], wo_ss.at[2], wo_rs.at[2], lane, pair)
     pl.semaphore_wait(barrier, 3 * seq_count - 1)
-    wo_far.start()
+    for copy in wo_far:
+        copy.start()
 
     loads[0].wait()
     loads[1].wait()
@@ -357,8 +365,8 @@
         ).wait_recv()
 
     blocks = cached // KEY_ROWS
-    for step in range(2):
-        chunk = 1 - own_chunk if step == 0 else own_chunk
+    def visit_chunk(step, carry):
+        chunk = lax.rem(own_chunk + 1 + step, 2)
         start = pl.multiple_of(chunk * QUERY_ROWS, QUERY_ROWS)
         q = queries[pl.ds(start, QUERY_ROWS), :]
 
@@ -377,8 +385,8 @@
         for b in range(blocks + 1):
             following = None
             if b < blocks:
-                if step == 0 and b == blocks - 1:
-                    take_new_entries()
+                if b == blocks - 1:
+                    pl.when(step == 0)(take_new_entries)
                 following = block_scores(b + 1)
             newer = current.max(axis=1, keepdims=True)
             if b > 0:
@@ -394,10 +402,15 @@
             lower = attn[t * positions + half : (t + 1) * positions, :]
             s = chunk * per_chunk + t
             ret_send[s] = jnp.where(lane_half, pltpu.roll(upper, 64, 1), lower).astype(bf16)
-            if step == 0:
-                ret_copy(0, s).start()
-                ret_copy(1, s).start()
-        if step == 1:
+
+        @pl.when(step == 0)
+        def _():
+            for t in range(per_chunk):
+                ret_copy(0, away_base + t).start()
+                ret_copy(1, away_base + t).start()
+
+        @pl.when(step == 1)
+        def _():
             for k in range(near_lanes):
                 s = near_base + lax.rem(lane + k, near_lanes)
                 for side in range(4):
@@ -405,8 +418,13 @@
                         ret_copy(side, s).start()
             ret[rep, lane] = ret_send[lane]
 
-    wo_far.wait_recv()
-    wo_pass.start()
+        return carry
+
+    lax.fori_loop(0, 2, visit_chunk, 0)
+
+    for h in range(2):
+        wo_far[h].wait_recv()
+        wo_pass[h].start()
 
     passes = []
     for side in (0, 1):
@@ -438,7 +456,8 @@
     wo_pair.wait_recv()
     passes[0].wait_recv()
     z_all[...] += project(pair)
-    wo_pass.wait_recv()
+    for copy in wo_pass:
+        copy.wait_recv()
     passes[1].wait_recv()
     z_all[...] += project(cross)
     z = z_all[...]
@@ -457,7 +476,7 @@
                 ret_copy(side, away_base + k).wait_send()
             if k or side:
                 ret_copy(side, near_base + lax.rem(lane + k, near_lanes)).wait_send()
-    for copy in [wo_far, wo_pair, wo_pass] + passes:
+    for copy in [wo_pair] + wo_far + wo_pass + passes:
         copy.wait_send()
 
 
@@ -516,8 +535,8 @@
             dma((seq_count,)),
             dma((seq_count,)),
             dma((seq_count,)),
-            dma((3,)),
-            dma((3,)),
+            dma((6,)),
+            dma((6,)),
             dma((4, seq_count)),
             dma((4, seq_count)),
             dma((2,)),

time: 29.7 us -> 29.4 us (0.990)
  Pallas kernels: 25.8 us -> 25.5 us
    pallas_call x1, Pallas kernels: 25.8 us -> 25.5 us  [fused(): pl.pallas_call(functools.partial(fused_kernel, seq_count), out_shape=(jax...]
where the time goes in v3:
time: 29.4 us; the launch traced here: 29.2 us
  Pallas kernels  25.5 us (87%)
  local copies, waits for them, and re-layouts  3.04 us (10%)
  between operations  0.64 us (2%)
    pallas_call x1, Pallas kernels, fused(): pl.pallas_call(functools.partial(fused_kernel, seq_count), out_shape=(jax...  25.5 us
    unnamed x2, local copies, waits for them, and re-layouts  3.04 us

profile of v3, /device:TPU:1, one launch (start us, length us, event | category | flops | bytes accessed | tf_op | source)
XLA Modules:
  0.0 29.2 jit_solution(2060011648511201539)
XLA Ops:
  0.6 25.5 %sublayer.1 = (bf16[128,256]{1,0:T(8,128)(2,1)}, bf16[512,128]{1,0:T(8,128)(2,1)}) custom-call(s32[2]{0:T(128)} %lengths_ref.1, s32[2]{0:T(128)} %counts_ref.1, bf16[128,1024]{1,0:T(8,128)(2,1)} %bitcast.5, bf16[1024,256]{1,0:T(8,128)(2,1)} %wq_hbm.1, bf16[1024,256]{1,0:T(8,128)(2,1)} %wk_hbm.1, bf16[1024,256]{1,0:T(8,128)(2,1)} %wv_hbm.1, ...), custom_call_target="tpu_custom_call" | custom-call | tf_op jit(solution)/shard_map/sublayer/pallas_call | solution.py:507
  26.2 1.5 %copy.14 = bf16[2,64,256]{2,1,0:T(8,128)(2,1)} copy(bf16[2,64,256]{2,1,0:T(8,128)(2,1)} %bitcast.7) | data formatting | bytes 131072
  27.6 1.6 %copy.15 = bf16[1,512,128]{2,1,0:T(8,128)(2,1)} copy(bf16[1,512,128]{2,1,0:T(8,128)(2,1)} %bitcast.6) | data formatting | bytes 262144
